TPU v7x, 32 devices: a whole 2x2x4 slice. The times are simulated.
32 devices in a mesh: ens: 2 (over y), band: 4 (over z), feat: 2 (over x), sub: 2 (over core).
Axes of the slice: x: 2, y: 2, z: 4, core: 2. Of those that a mesh axis runs over, the one named last changes fastest.
Arguments:
- grid_state: bfloat16 [16384, 512], P(('ens', 'band', 'feat', 'sub')), parts along dimension 0, may hold values from -6 to 6
- mesh_state: bfloat16 [16384, 512], P(('ens', 'band', 'feat', 'sub')), parts along dimension 0, may hold values from -6 to 6
- g2m_sender: int32 [16384], P(('band', 'feat', 'sub')), may hold values from 0 to 511
- g2m_slot: int32 [16384], P(('band', 'feat', 'sub')), may hold values from 0 to 383, as said below
- g2m_land: int32 [6144], P(('band', 'feat', 'sub')), may hold values from 0 to 511
- mesh_sender: int32 [32768], P(('band', 'feat', 'sub')), may hold values from 0 to 767
- mesh_receiver: int32 [32768], P(('band', 'feat', 'sub')), may hold values from 0 to 511
- m2g_sender: int32 [24576], P(('band', 'feat', 'sub')), may hold values from 0 to 767
- m2g_receiver: int32 [24576], P(('band', 'feat', 'sub')), may hold values from 0 to 511
- enc_msg_w1: bfloat16 [512, 512], P('band'), may hold values from -0.25 to 0.25
- enc_msg_b1: float32 [512], replicated, may hold values from -3 to 3
- enc_msg_w2: bfloat16 [512, 512], P('band'), may hold values from -0.25 to 0.25
- enc_node_w1: bfloat16 [1024, 512], P('band'), may hold values from -0.1875 to 0.1875
- enc_node_b1: float32 [512], replicated, may hold values from -3 to 3
- enc_node_w2: bfloat16 [512, 512], P('band'), may hold values from -0.25 to 0.25
- enc_gain: float32 [512], replicated, may hold values from 0.1 to 1.9
- proc_msg_w1: bfloat16 [1, 1024, 512], P(None, 'band'), may hold values from -0.1875 to 0.1875
- proc_msg_b1: float32 [1, 512], replicated, may hold values from -3 to 3
- proc_msg_w2: bfloat16 [1, 512, 512], P(None, 'band'), may hold values from -0.25 to 0.25
- proc_node_w1: bfloat16 [1, 1024, 512], P(None, 'band'), may hold values from -0.1875 to 0.1875
- proc_node_b1: float32 [1, 512], replicated, may hold values from -3 to 3
- proc_node_w2: bfloat16 [1, 512, 512], P(None, 'band'), may hold values from -0.25 to 0.25
- proc_gain: float32 [1, 512], replicated, may hold values from 0.1 to 1.9
- dec_msg_w1: bfloat16 [1024, 512], P('band'), may hold values from -0.1875 to 0.1875
- dec_msg_b1: float32 [512], replicated, may hold values from -3 to 3
- dec_msg_w2: bfloat16 [512, 512], P('band'), may hold values from -0.25 to 0.25
- dec_node_w1: bfloat16 [1024, 512], P('band'), may hold values from -0.1875 to 0.1875
- dec_node_b1: float32 [512], replicated, may hold values from -3 to 3
- dec_node_w2: bfloat16 [512, 512], P('band'), may hold values from -0.25 to 0.25
- dec_gain: float32 [512], replicated, may hold values from 0.1 to 1.9
Outputs:
- grid_next: bfloat16 [16384, 512], P(('ens', 'band', 'feat', 'sub')), parts along dimension 0
There are 2 independent parts, one for each index of `ens`. A program takes and returns all parts, laid end to end along the dimension named above; an argument that names none is the same for every part. Nothing has to cross between parts.
Inputs may be any that keep to these rules, and one draw needn't show every extreme that they name: `g2m_sender`: A grid row among the 512 rows of the edge's own device. `g2m_slot`: slot k * 128 + c of a device (k = 0, 1, 2) goes to the device k - 1 places further along band+feat+sub. The first device uses no slot with k = 0 and the last none with k = 2; every other slot of a device is used by one edge or more. `g2m_land`: entry k * 128 + c of a device's block: its own mesh row where slot k * 128 + c of the device k - 1 places before it lands. `mesh_sender`: A row of the device's extended mesh rows: the previous device's last 128 mesh rows, its own 512, the next device's first 128; rows beyond the whole mesh are zero. `mesh_receiver`: A mesh row among the device's own 512. `m2g_sender`: A row of the device's extended mesh rows, as for mesh_sender. `m2g_receiver`: A grid row among the device's own 512.
All inputs are finite; a program needn't handle non-finite values.
Results may differ from a plain program's by a relative error of at most 0.0095.
Values may be sent and summed in bfloat16 or wider, within the bound.
A program may use at most 64 MiB of HBM per device.

v0:
```python
import jax
import jax.numpy as jnp
from jax import lax
from jax.sharding import PartitionSpec as P

HALO = 128


def with_halo(cells, sides, width):
    for axis, dim in sides:
        count = lax.axis_size(axis)
        ends = count - 1
        head = lax.slice_in_dim(cells, 0, width, axis=dim)
        tail = lax.slice_in_dim(cells, cells.shape[dim] - width, cells.shape[dim], axis=dim)
        cells = jnp.concatenate(
            [
                lax.ppermute(tail, axis, [(i, (i + 1) % count) for i in range(ends)]),
                cells,
                lax.ppermute(head, axis, [((i + 1) % count, i) for i in range(ends)]),
            ],
            axis=dim,
        )
    return cells


def layer_norm(values, gain_row):
    average = jnp.mean(values, axis=1, keepdims=True)
    centred = values - average
    spread = jnp.mean(centred * centred, axis=1, keepdims=True)
    return centred * lax.rsqrt(spread + 1e-05) * gain_row


def node_update(latent, summed, message_out, node_in, node_bias, node_out, gain_row):
    model_width = latent.shape[1]
    summed_narrow = summed.astype(jnp.bfloat16)
    incoming = jnp.dot(summed_narrow, message_out, preferred_element_type=jnp.float32)
    incoming_narrow = incoming.astype(jnp.bfloat16)
    before = jnp.dot(latent, node_in[:model_width], preferred_element_type=jnp.float32)
    before = (
        before
        + jnp.dot(incoming_narrow, node_in[model_width:], preferred_element_type=jnp.float32)
        + node_bias
    )
    hidden = jax.nn.silu(before).astype(jnp.bfloat16)
    mixed_out = jnp.dot(hidden, node_out, preferred_element_type=jnp.float32)
    return (latent.astype(jnp.float32) + layer_norm(mixed_out, gain_row)).astype(jnp.bfloat16)


def fetch_section(first, second, third, fourth):
    return (
        lax.all_gather(first, "band", axis=0, tiled=True),
        lax.all_gather(second, "band", axis=0, tiled=True),
        lax.all_gather(third, "band", axis=0, tiled=True),
        lax.all_gather(fourth, "band", axis=0, tiled=True),
    )


def mesh_rim(latent):
    return with_halo(latent, ((("band", "feat", "sub"), 0),), HALO)


def edge_sum(framed_terms, target_terms, senders, receivers, unit_bias, row_count):
    before = (
        jnp.take(framed_terms, senders, axis=0)
        + jnp.take(target_terms, receivers, axis=0)
        + unit_bias
    )
    return jax.ops.segment_sum(jax.nn.silu(before), receivers, num_segments=row_count)


def on_device(
    grid_state,
    mesh_state,
    g2m_sender,
    g2m_slot,
    g2m_land,
    mesh_sender,
    mesh_receiver,
    m2g_sender,
    m2g_receiver,
    enc_msg_w1,
    enc_msg_b1,
    enc_msg_w2,
    enc_node_w1,
    enc_node_b1,
    enc_node_w2,
    enc_gain,
    proc_msg_w1,
    proc_msg_b1,
    proc_msg_w2,
    proc_node_w1,
    proc_node_b1,
    proc_node_w2,
    proc_gain,
    dec_msg_w1,
    dec_msg_b1,
    dec_msg_w2,
    dec_node_w1,
    dec_node_b1,
    dec_node_w2,
    dec_gain,
):
    model_width = grid_state.shape[1]
    grid_count = grid_state.shape[0]
    mesh_count = mesh_state.shape[0]
    capacity = g2m_land.shape[0] // 3
    enc_set = fetch_section(enc_msg_w1, enc_msg_w2, enc_node_w1, enc_node_w2)
    proc_sets = fetch_section(proc_msg_w1[0], proc_msg_w2[0], proc_node_w1[0], proc_node_w2[0])
    dec_set = fetch_section(dec_msg_w1, dec_msg_w2, dec_node_w1, dec_node_w2)
    grid_hidden = jax.nn.silu(
        jnp.dot(grid_state, enc_set[0], preferred_element_type=jnp.float32) + enc_msg_b1
    )
    hidden_cols = grid_hidden.shape[1]
    edge_terms = jnp.take(grid_hidden, g2m_sender, axis=0)
    blocks = jax.ops.segment_sum(edge_terms, g2m_slot, num_segments=3 * capacity).reshape(
        3, capacity, hidden_cols
    )
    outgoing = jnp.concatenate([blocks[0], blocks[2]], axis=0)
    framed_pair = with_halo(outgoing, ((("band", "feat", "sub"), 0),), capacity)
    incoming = jnp.stack([framed_pair[3 * capacity :], blocks[1], framed_pair[:capacity]], axis=0)
    enc_hidden = jax.ops.segment_sum(
        incoming.reshape(3 * capacity, hidden_cols), g2m_land, num_segments=mesh_count
    )
    mesh_latent = node_update(
        mesh_state, enc_hidden, enc_set[1], enc_set[2], enc_node_b1, enc_set[3], enc_gain
    )
    weights_in, message_out, node_in, node_out = proc_sets
    framed = mesh_rim(mesh_latent)
    framed_terms = jnp.dot(framed, weights_in[:model_width], preferred_element_type=jnp.float32)
    local_terms = jnp.dot(mesh_latent, weights_in[model_width:], preferred_element_type=jnp.float32)
    proc_hidden = edge_sum(
        framed_terms, local_terms, mesh_sender, mesh_receiver, proc_msg_b1[0], mesh_count
    )
    mesh_latent = node_update(
        mesh_latent, proc_hidden, message_out, node_in, proc_node_b1[0], node_out, proc_gain[0]
    )
    framed = mesh_rim(mesh_latent)
    framed_terms = jnp.dot(framed, dec_set[0][:model_width], preferred_element_type=jnp.float32)
    grid_terms = jnp.dot(grid_state, dec_set[0][model_width:], preferred_element_type=jnp.float32)
    dec_hidden = edge_sum(
        framed_terms, grid_terms, m2g_sender, m2g_receiver, dec_msg_b1, grid_count
    )
    return node_update(
        grid_state, dec_hidden, dec_set[1], dec_set[2], dec_node_b1, dec_set[3], dec_gain
    )


def solution(mesh):
    in_specs = (
        P(("ens", "band", "feat", "sub"), None),
        P(("ens", "band", "feat", "sub"), None),
        P(("band", "feat", "sub")),
        P(("band", "feat", "sub")),
        P(("band", "feat", "sub")),
        P(("band", "feat", "sub")),
        P(("band", "feat", "sub")),
        P(("band", "feat", "sub")),
        P(("band", "feat", "sub")),
        P("band", None),
        P(),
        P("band", None),
        P("band", None),
        P(),
        P("band", None),
        P(),
        P(None, "band", None),
        P(),
        P(None, "band", None),
        P(None, "band", None),
        P(),
        P(None, "band", None),
        P(),
        P("band", None),
        P(),
        P("band", None),
        P("band", None),
        P(),
        P("band", None),
        P(),
    )
    out_specs = P(("ens", "band", "feat", "sub"), None)
    return jax.shard_map(
        on_device, mesh=mesh, in_specs=in_specs, out_specs=out_specs, check_vma=False
    )
```

profile of v0, /device:TPU:3, one launch (start us, length us, event | category | flops | bytes accessed | tf_op | source)
XLA Modules:
  0.0 286.8 jit_solution(2307445052972402567)
XLA Ops:
  9.4 16.2 %all_gather.38 = bf16[512,512]{1,0:T(8,128)(2,1)S(1)} all-gather(bf16[128,512]{1,0:T(8,128)(2,1)} %param.39), channel_id=1, replica_groups=mesh['ens'=2,'band'=4,'feat'=2,'sub'=2] {'band'}, dimensions={0}, use_global_device_ids=true | all-gather | bytes 655360 | tf_op jit(solution)/shard_map/all_gather | solution.py:51
  26.2 11.4 %scatter_custom_fusion = f32[384,512]{1,0:T(8,128)S(1)} fusion(s32[1024]{0:T(1024)} %param.33, f32[]{:T(128)} %constant.87.clone.1, pred[1024]{0:T(1024)(128)(4,1)S(1)} %compare_and_fusion.4, f32[]{:T(128)} %constant.80.clone.1, f32[512,512]{1,0:T(8,128)S(1)} %divide_multiply_fusion, s32[1024]{0:T(1024)S(1)} %fusion.77), kind=kCustom, calls=%fused_computation.32 | custom fusion | flops 1048576 | bytes 1841152 | tf_op jit(solution)/shard_map/scatter-add | solution.py:115
  37.8 7.3 %collective-permute-start = (f32[128,512]{1,0:T(8,128)S(1)}, f32[128,512]{1,0:T(8,128)S(1)}, u32[]{:S(2)}, u32[]{:S(2)}) collective-permute-start(f32[128,512]{1,0:T(8,128)S(1)} %get-tuple-element.5), channel_id=1, source_target_pairs={{1,0},{2,1},{3,2},{4,3},{5,4},{6,5},{7,6},{8,7},{9,8},{10,9},{11,1... | collective-permute-start | bytes 786440 | tf_op jit(solution)/shard_map/ppermute | solution.py:19
  47.1 19.0 %all_gather.39 = bf16[512,512]{1,0:T(8,128)(2,1)} all-gather(bf16[128,512]{1,0:T(8,128)(2,1)S(1)} %copy-done.10), channel_id=1, replica_groups=mesh['ens'=2,'band'=4,'feat'=2,'sub'=2] {'band'}, dimensions={0}, use_global_device_ids=true | all-gather | bytes 655360 | tf_op jit(solution)/shard_map/all_gather | solution.py:52
  66.1 19.1 %all_gather.40 = bf16[512,512]{1,0:T(8,128)(2,1)S(1)} all-gather(bf16[128,512]{1,0:T(8,128)(2,1)S(1)} %copy-done.11), channel_id=1, replica_groups=mesh['ens'=2,'band'=4,'feat'=2,'sub'=2] {'band'}, dimensions={0}, use_global_device_ids=true | all-gather | bytes 655360 | tf_op jit(solution)/shard_map/all_gather | solution.py:54
  85.2 15.0 %all-gather.2 = bf16[1,512,512]{2,1,0:T(8,128)(2,1)} all-gather(bf16[1,128,512]{2,1,0:T(8,128)(2,1)S(1)} %copy-done.12), channel_id=4, replica_groups=mesh['ens'=2,'band'=4,'feat'=2,'sub'=2] {'band'}, dimensions={1}, use_global_device_ids=true | all-gather | bytes 655360 | tf_op jit(solution)/shard_map/all_gather | solution.py:52
  100.2 21.4 %all-gather.3 = bf16[1,512,512]{2,1,0:T(8,128)(2,1)} all-gather(bf16[1,128,512]{2,1,0:T(8,128)(2,1)S(1)} %copy-done.13), channel_id=5, replica_groups=mesh['ens'=2,'band'=4,'feat'=2,'sub'=2] {'band'}, dimensions={1}, use_global_device_ids=true | all-gather | bytes 655360 | tf_op jit(solution)/shard_map/all_gather | solution.py:54
  121.6 14.2 %all_gather.46 = bf16[512,512]{1,0:T(8,128)(2,1)} all-gather(bf16[128,512]{1,0:T(8,128)(2,1)S(1)} %copy-done.14), channel_id=1, replica_groups=mesh['ens'=2,'band'=4,'feat'=2,'sub'=2] {'band'}, dimensions={0}, use_global_device_ids=true | all-gather | bytes 655360 | tf_op jit(solution)/shard_map/all_gather | solution.py:52
  135.8 21.3 %all_gather.47 = bf16[512,512]{1,0:T(8,128)(2,1)} all-gather(bf16[128,512]{1,0:T(8,128)(2,1)S(1)} %copy-done.15), channel_id=1, replica_groups=mesh['ens'=2,'band'=4,'feat'=2,'sub'=2] {'band'}, dimensions={0}, use_global_device_ids=true | all-gather | bytes 655360 | tf_op jit(solution)/shard_map/all_gather | solution.py:54
  159.9 3.2 %scatter_custom_fusion.1 = f32[512,512]{1,0:T(8,128)S(1)} fusion(s32[384]{0:T(512)} %param.34, f32[384,512]{1,0:T(8,128)S(1)} %bitcast.43, f32[]{:T(128)} %constant.80.clone.1), kind=kCustom, calls=%fused_computation.99 | custom fusion | flops 196608 | bytes 1049088 | tf_op jit(solution)/shard_map/scatter-add | solution.py:121
  163.2 2.5 fusion.56
  165.6 2.4 multiply_convert_fusion.2
  169.2 15.4 %collective-permute-start.2 = (bf16[128,512]{1,0:T(8,128)(2,1)S(1)}, bf16[128,512]{1,0:T(8,128)(2,1)}, u32[]{:S(2)}, u32[]{:S(2)}) collective-permute-start(bf16[128,512]{1,0:T(8,128)(2,1)S(1)} %get-tuple-element.10), channel_id=1, source_target_pairs={{0,1},{1,2},{2,3},{3,4},{4,5},{5,6},{6,7},{7,8},{8,9},{9,10},{10,1... | collective-permute-start | bytes 393224 | tf_op jit(solution)/shard_map/ppermute | solution.py:17
  184.6 2.1 collective-permute-start.3
  188.2 2.5 fusion.54
  192.3 2.7 fusion.37
  195.1 35.8 %scatter_custom_fusion.2 = f32[512,512]{1,0:T(8,128)} fusion(s32[2048]{0:T(1024)S(1)} %copy-done.19, f32[]{:T(128)} %constant.86.clone.1, f32[512]{0:T(512)S(1)} %bitcast.46, f32[]{:T(128)} %constant.87.clone.1, pred[2048]{0:T(1024)(128)(4,1)S(1)} %get-tuple-element.18, pred[2048]{0:T(1024)(128)(4,1)S(1)} %get-tuple-element.19, f32[]{:T(128)} %constant.80.clone.1, ...), kind=kCustom, calls=%fused_computation.9 | custom fusion | flops 9437184 | bytes 3692556 | tf_op jit(solution)/shard_map/scatter-add | solution.py:68
  230.8 2.8 multiply_convert_fusion.1
  238.1 4.5 %collective-permute-start.4 = (bf16[128,512]{1,0:T(8,128)(2,1)S(1)}, bf16[128,512]{1,0:T(8,128)(2,1)S(1)}, u32[]{:S(2)}, u32[]{:S(2)}) collective-permute-start(bf16[128,512]{1,0:T(8,128)(2,1)S(1)} %get-tuple-element.8), channel_id=1, source_target_pairs={{0,1},{1,2},{2,3},{3,4},{4,5},{5,6},{6,7},{7,8},{8,9},{9,10},{10,1... | collective-permute-start | bytes 393224 | tf_op jit(solution)/shard_map/ppermute | solution.py:17
  242.6 2.1 collective-permute-start.5
  244.8 2.5 fusion.58
  247.3 2.5 collective-permute-done.5
  251.5 23.9 %scatter_custom_fusion.3 = f32[512,512]{1,0:T(8,128)} fusion(s32[1536]{0:T(1024)S(1)} %copy-done.17, f32[]{:T(128)} %constant.86.clone.1, f32[512]{0:T(512)S(1)} %copy-done.22, f32[]{:T(128)} %constant.87.clone.1, pred[1536]{0:T(1024)(128)(4,1)S(1)} %get-tuple-element.24, pred[1536]{0:T(1024)(128)(4,1)S(1)} %get-tuple-element.25, f32[]{:T(128)} %constant.80.clone.1, ...), kind=kCustom, calls=%fused_computation.19 | custom fusion | flops 7077888 | bytes 3692556 | tf_op jit(solution)/shard_map/scatter-add | solution.py:68
  275.3 2.6 multiply_convert_fusion
  (115 shorter events, 20.7 us)
Async XLA Ops:
  6.5 156.6 %all-gather.12.cloned.1.call-start = ((), (), s32[]{:S(2)}) async-start(), calls=%async_computation.1 | async-start | bytes 1310720 | tf_op jit(solution)/shard_map/all_gather | solution.py:53
  7.3 179.4 %all-gather.18.cloned.1.call-start = ((), (), s32[]{:S(2)}) async-start(), calls=%async_computation.4 | async-start | bytes 1310720 | tf_op jit(solution)/shard_map/all_gather | solution.py:51
  8.0 180.2 %all-gather.16.cloned.1.call-start = ((), (), s32[]{:S(2)}) async-start(), calls=%async_computation.3 | async-start | bytes 1310720 | tf_op jit(solution)/shard_map/all_gather | solution.py:53
  8.7 182.0 %all-gather.14.cloned.1.call-start = ((), (), s32[]{:S(2)}) async-start(), calls=%async_computation.2 | async-start | bytes 1310720 | tf_op jit(solution)/shard_map/all_gather | solution.py:51
  9.3 235.5 %all-gather.10.cloned.1.call-start = ((), (), s32[]{:S(2)}) async-start(), calls=%async_computation | async-start | bytes 1310720 | tf_op jit(solution)/shard_map/all_gather | solution.py:53
  26.2 20.8 %copy-start.17 = (s32[1536]{0:T(1024)S(1)}, s32[1536]{0:T(1024)}, u32[]{:S(2)}) copy-start(s32[1536]{0:T(1024)} %param.38) | copy-start | bytes 18436
  26.2 20.8 %copy-start.16 = (s32[1536]{0:T(1024)S(1)}, s32[1536]{0:T(1024)}, u32[]{:S(2)}) copy-start(s32[1536]{0:T(1024)} %param.37) | copy-start | bytes 18436
  26.2 20.8 %copy-start.10 = (bf16[128,512]{1,0:T(8,128)(2,1)S(1)}, bf16[128,512]{1,0:T(8,128)(2,1)}, u32[]{:S(2)}) copy-start(bf16[128,512]{1,0:T(8,128)(2,1)} %param.41) | copy-start | bytes 393220
  37.6 28.4 %copy-start.11 = (bf16[128,512]{1,0:T(8,128)(2,1)S(1)}, bf16[128,512]{1,0:T(8,128)(2,1)}, u32[]{:S(2)}) copy-start(bf16[128,512]{1,0:T(8,128)(2,1)} %param.44) | copy-start | bytes 393220
  37.7 47.6 %copy-start.12 = (bf16[1,128,512]{2,1,0:T(8,128)(2,1)S(1)}, bf16[1,128,512]{2,1,0:T(8,128)(2,1)}, u32[]{:S(2)}) copy-start(bf16[1,128,512]{2,1,0:T(8,128)(2,1)} %param.48) | copy-start | bytes 393220
  37.7 62.6 %copy-start.13 = (bf16[1,128,512]{2,1,0:T(8,128)(2,1)S(1)}, bf16[1,128,512]{2,1,0:T(8,128)(2,1)}, u32[]{:S(2)}) copy-start(bf16[1,128,512]{2,1,0:T(8,128)(2,1)} %param.51) | copy-start | bytes 393220
  37.7 83.8 %copy-start.14 = (bf16[128,512]{1,0:T(8,128)(2,1)S(1)}, bf16[128,512]{1,0:T(8,128)(2,1)}, u32[]{:S(2)}) copy-start(bf16[128,512]{1,0:T(8,128)(2,1)} %param.55) | copy-start | bytes 393220
  37.8 120.4 %collective-permute-start = (f32[128,512]{1,0:T(8,128)S(1)}, f32[128,512]{1,0:T(8,128)S(1)}, u32[]{:S(2)}, u32[]{:S(2)}) collective-permute-start(f32[128,512]{1,0:T(8,128)S(1)} %get-tuple-element.5), channel_id=1, source_target_pairs={{1,0},{2,1},{3,2},{4,3},{5,4},{6,5},{7,6},{8,7},{9,8},{10,9},{11,1... | collective-permute-start | bytes 786440 | tf_op jit(solution)/shard_map/ppermute | solution.py:19
  45.0 113.1 %collective-permute-start.1 = (f32[128,512]{1,0:T(8,128)S(1)}, f32[128,512]{1,0:T(8,128)S(1)}, u32[]{:S(2)}, u32[]{:S(2)}) collective-permute-start(f32[128,512]{1,0:T(8,128)S(1)} %get-tuple-element.6), channel_id=1, source_target_pairs={{0,1},{1,2},{2,3},{3,4},{4,5},{5,6},{6,7},{7,8},{8,9},{9,10},{10,1... | collective-permute-start | bytes 786440 | tf_op jit(solution)/shard_map/ppermute | solution.py:17
  47.1 88.7 %copy-start.15 = (bf16[128,512]{1,0:T(8,128)(2,1)S(1)}, bf16[128,512]{1,0:T(8,128)(2,1)}, u32[]{:S(2)}) copy-start(bf16[128,512]{1,0:T(8,128)(2,1)} %param.58) | copy-start | bytes 393220
  66.1 91.0 %copy-start.18 = (s32[2048]{0:T(1024)S(1)}, s32[2048]{0:T(1024)}, u32[]{:S(2)}) copy-start(s32[2048]{0:T(1024)} %param.35) | copy-start | bytes 24580
  66.1 91.0 %copy-start.19 = (s32[2048]{0:T(1024)S(1)}, s32[2048]{0:T(1024)}, u32[]{:S(2)}) copy-start(s32[2048]{0:T(1024)} %param.36) | copy-start | bytes 24580
  169.2 23.1 %collective-permute-start.2 = (bf16[128,512]{1,0:T(8,128)(2,1)S(1)}, bf16[128,512]{1,0:T(8,128)(2,1)}, u32[]{:S(2)}, u32[]{:S(2)}) collective-permute-start(bf16[128,512]{1,0:T(8,128)(2,1)S(1)} %get-tuple-element.10), channel_id=1, source_target_pairs={{0,1},{1,2},{2,3},{3,4},{4,5},{5,6},{6,7},{7,8},{8,9},{9,10},{10,1... | collective-permute-start | bytes 393224 | tf_op jit(solution)/shard_map/ppermute | solution.py:17
  184.6 7.7 %collective-permute-start.3 = (bf16[128,512]{1,0:T(8,128)(2,1)S(1)}, bf16[128,512]{1,0:T(8,128)(2,1)}, u32[]{:S(2)}, u32[]{:S(2)}) collective-permute-start(bf16[128,512]{1,0:T(8,128)(2,1)S(1)} %get-tuple-element.11), channel_id=1, source_target_pairs={{1,0},{2,1},{3,2},{4,3},{5,4},{6,5},{7,6},{8,7},{9,8},{10,9},{11,1... | collective-permute-start | bytes 393224 | tf_op jit(solution)/shard_map/ppermute | solution.py:19
  195.1 35.8 %copy-start.28 = (f32[1,512]{1,0:T(1,128)S(1)}, f32[1,512]{1,0:T(1,128)}, u32[]{:S(2)}) copy-start(f32[1,512]{1,0:T(1,128)} %param.50) | copy-start | bytes 6148
  238.1 9.3 %collective-permute-start.4 = (bf16[128,512]{1,0:T(8,128)(2,1)S(1)}, bf16[128,512]{1,0:T(8,128)(2,1)S(1)}, u32[]{:S(2)}, u32[]{:S(2)}) collective-permute-start(bf16[128,512]{1,0:T(8,128)(2,1)S(1)} %get-tuple-element.8), channel_id=1, source_target_pairs={{0,1},{1,2},{2,3},{3,4},{4,5},{5,6},{6,7},{7,8},{8,9},{9,10},{10,1... | collective-permute-start | bytes 393224 | tf_op jit(solution)/shard_map/ppermute | solution.py:17
  242.6 7.2 %collective-permute-start.5 = (bf16[128,512]{1,0:T(8,128)(2,1)S(1)}, bf16[128,512]{1,0:T(8,128)(2,1)S(1)}, u32[]{:S(2)}, u32[]{:S(2)}) collective-permute-start(bf16[128,512]{1,0:T(8,128)(2,1)S(1)} %get-tuple-element.9), channel_id=1, source_target_pairs={{1,0},{2,1},{3,2},{4,3},{5,4},{6,5},{7,6},{8,7},{9,8},{10,9},{11,1... | collective-permute-start | bytes 393224 | tf_op jit(solution)/shard_map/ppermute | solution.py:19
  251.4 23.9 %copy-start.7 = (bf16[512,512]{1,0:T(8,128)(2,1)S(1)}, bf16[512,512]{1,0:T(8,128)(2,1)}, u32[]{:S(2)}) copy-start(bf16[512,512]{1,0:T(8,128)(2,1)} %all_gather.46) | copy-start | bytes 1572868
  251.4 23.9 %copy-start.29 = (f32[512]{0:T(512)S(1)}, f32[512]{0:T(512)}, u32[]{:S(2)}) copy-start(f32[512]{0:T(512)} %param.57) | copy-start | bytes 6148
  (17 other events, 93.1 us)
Sparse Core Ops, SparseCore 0:
  8.9 32.5 all-gather.11
  43.1 38.9 all-gather.17
  83.7 40.0 all-gather.15
  125.2 37.0 all-gather.13
  163.7 27.4 all-gather.9
where the time goes:
time: 288 us; the launch traced here: 287 us
  blocking collectives  126 us (44%)
  other arithmetic  76.8 us (27%)
  starting transfers between devices  33.5 us (12%)
  matrix products  25.8 us (9%)
  between operations  13.7 us (5%)
  local copies, waits for them, and re-layouts  5.63 us (2%)
  waiting for transfers between devices  5.2 us (2%)
    all_gather x3, blocking collectives, fetch_section(): lax.all_gather(fourth, 'band', axis=0, tiled=True)  61.8 us
    scatter-add x2, other arithmetic, edge_sum(): jax.ops.segment_sum(jax.nn.silu(before), receivers, num_segments=row_count)  59.6 us
    all_gather x3, blocking collectives, fetch_section(): lax.all_gather(second, 'band', axis=0, tiled=True)  48.2 us
    ppermute x3, starting transfers between devices, with_halo(): lax.ppermute(tail, axis, [(i, (i + 1) % count) for i in range(ends)])  21.8 us
    all_gather x1, blocking collectives, fetch_section(): lax.all_gather(first, 'band', axis=0, tiled=True)  16.2 us
    ppermute x3, starting transfers between devices, with_halo(): lax.ppermute(head, axis, [((i + 1) % count, i) for i in range(ends)])  11.5 us
    scatter-add x1, other arithmetic, on_device(): jax.ops.segment_sum(edge_terms, g2m_slot, num_segments=3 * capacity)  11.4 us
    dot_general x3, matrix products, node_update(): jnp.dot(incoming_narrow, node_in[model_width:], preferred_element_type=jn...  7.8 us
  transfers between devices with their start and end apart: 11, of which 1 were waited for; matrix products, arithmetic and copies ran while one was open for 27% of the time, Pallas kernels for 0%

commit v1 on v0

v1 whole, which is shorter than its diff:
```python
import functools

import jax
import jax.numpy as jnp
from jax import lax
from jax.experimental import pallas as pl
from jax.experimental.pallas import tpu as pltpu
from jax.sharding import PartitionSpec as P

HALO = 128
LANES = 128
F32 = jnp.float32
BF16 = jnp.bfloat16
MESH = pl.DeviceIdType.MESH

GROUPS = ((0,), (1, 2, 3), (4, 5, 6, 7), (8, 9, 10, 11))


def silu(v):
    h = 0.5 * v
    return h + h * jnp.tanh(h)


def dot(a, b):
    return jnp.dot(a, b, preferred_element_type=F32)


def kernel(dims, plan, *refs):
    bands, feats, subs = dims
    (
        grid_hbm, mesh_hbm, g2m_s, g2m_q, g2m_l, mesh_s, mesh_r, m2g_s, m2g_r,
        enc_b1, enc_nb, enc_gain, proc_b1, proc_nb, proc_gain, dec_b1, dec_nb, dec_gain,
    ) = refs[:18]
    shards = refs[18:30]
    out_ref = refs[30]
    (
        w0, w1, w2, w3, grid, mesh, inc, slots_out, framed_a, framed_b, counts,
        oh_g, oht_q, land, oh_m, oht_m, oh_d, oht_d, terms, terms_d, msg,
        zsend, zrecv, psend, precv, dsend, drecv, wsem, ssem, hsend, hrecv,
    ) = refs[31:]
    wbufs = (w0, w1, w2, w3)
    y = lax.axis_index("ens")
    z = lax.axis_index("band")
    x = lax.axis_index("feat")
    c = lax.axis_index("sub")
    xn = x + 1 - 2 * lax.rem(x, 2)
    yn = 1 - y
    q = 2 * y + lax.rem(x, 2)
    position = (z * feats + x) * subs + c
    last = bands * feats * subs - 1
    has_left = position > 0
    has_right = position < last

    def place(number):
        return (y, number // (feats * subs), lax.rem(number // subs, feats), lax.rem(number, subs))

    left = place(lax.rem(position + last, last + 1))
    right = place(lax.rem(position + 1, last + 1))
    sibling = (y, z, x, 1 - c)
    peers = ((y, z, xn, c), (yn, z, x, c), (yn, z, xn, c))
    chunks = (2 * y + lax.rem(xn, 2), 2 * yn + lax.rem(x, 2), 2 * yn + lax.rem(xn, 2))

    local = []
    for g, members in enumerate(GROUPS):
        group = []
        for m in members:
            off, rows = plan[m]
            group.append(
                pltpu.make_async_copy(
                    shards[m], wbufs[g].at[z, pl.ds(off, rows), :], wsem.at[m]
                )
            )
        local.append(group)
    states = (
        pltpu.make_async_copy(grid_hbm, grid, ssem.at[0]),
        pltpu.make_async_copy(mesh_hbm, mesh, ssem.at[1]),
    )
    for group in local:
        for copy in group:
            copy.start()
    for copy in states:
        copy.start()

    barrier = pltpu.get_barrier_semaphore()

    def greet(r, carry):
        pl.semaphore_signal(
            barrier, inc=1, device_id=(y, lax.rem(z + r, bands), x, c), device_id_type=MESH
        )
        return carry

    lax.fori_loop(1, bands, greet, 0)
    for peer in peers:
        pl.semaphore_signal(barrier, inc=1, device_id=peer, device_id_type=MESH)
    for peer in (sibling, left, right):
        pl.semaphore_signal(barrier, inc=1, device_id=peer, device_id_type=MESH)
    pl.semaphore_wait(barrier, bands - 1 + 6)

    def half_rows(g, core):
        half = wbufs[g].shape[1] // 2
        return pl.ds(pl.multiple_of(core * half, 16), half)

    def cols(chunk):
        width = wbufs[0].shape[2] // 4
        return pl.ds(pl.multiple_of(chunk * width, LANES), width)

    def z_copy(g, r, owner, target):
        piece = wbufs[g].at[owner, half_rows(g, c), cols(q)]
        return pltpu.make_async_remote_copy(
            piece, piece, zsend.at[g, r], zrecv.at[g, r],
            device_id=(y, target, x, c), device_id_type=MESH,
        )

    def p_copy(g, r, owner, j, chunk):
        piece = wbufs[g].at[owner, half_rows(g, c), cols(chunk)]
        return pltpu.make_async_remote_copy(
            piece, piece, psend.at[g, r, j], precv.at[g, r, j],
            device_id=peers[j], device_id_type=MESH,
        )

    def d_copy(g, r, owner, core):
        piece = wbufs[g].at[owner, half_rows(g, core), :]
        return pltpu.make_async_remote_copy(
            piece, piece, dsend.at[g, r], drecv.at[g, r],
            device_id=sibling, device_id_type=MESH,
        )

    def each(body):
        def step(r, carry):
            body(r, lax.rem(z - r + bands, bands))
            return carry

        lax.fori_loop(1, bands, step, 0)

    def z_start(g):
        for copy in local[g]:
            copy.wait()
        each(lambda r, owner: z_copy(g, r, z, lax.rem(z + r, bands)).start())

    def z_pass(g):
        def body(r, owner):
            z_copy(g, r, owner, owner).wait_recv()
            for j in range(3):
                p_copy(g, r, owner, j, q).start()

        each(body)

    def p_pass(g):
        def body(r, owner):
            for j in range(3):
                p_copy(g, r, owner, j, chunks[j]).wait_recv()
            d_copy(g, r, owner, c).start()

        each(body)

    def d_wait(g):
        each(lambda r, owner: d_copy(g, r, owner, 1 - c).wait_recv())

    def finish(g):
        def body(r, owner):
            z_copy(g, r, z, lax.rem(z + r, bands)).wait_send()
            for j in range(3):
                p_copy(g, r, owner, j, q).wait_send()
            d_copy(g, r, owner, c).wait_send()

        each(body)

    def weight(g, m, first=0, count=None):
        off, rows = plan[m]
        whole = wbufs[g][:, off : off + rows, :]
        return whole.reshape(bands * rows, whole.shape[2])

    def exchange(step, to_left, from_right, to_right, from_left):
        def left_copy():
            return pltpu.make_async_remote_copy(
                to_left, from_right, hsend.at[step, 0], hrecv.at[step, 0],
                device_id=left, device_id_type=MESH,
            )

        def right_copy():
            return pltpu.make_async_remote_copy(
                to_right, from_left, hsend.at[step, 1], hrecv.at[step, 1],
                device_id=right, device_id_type=MESH,
            )

        def start():
            @pl.when(has_left)
            def _():
                left_copy().start()

            @pl.when(has_right)
            def _():
                right_copy().start()

        def wait():
            @pl.when(has_right)
            def _():
                left_copy().wait_recv()

            @pl.when(has_left)
            def _():
                right_copy().wait_recv()

        def done():
            @pl.when(has_left)
            def _():
                left_copy().wait_send()

            @pl.when(has_right)
            def _():
                right_copy().wait_send()

        return start, wait, done

    cap = inc.shape[0] // 3
    rows_m = mesh.shape[0]
    width = mesh.shape[1]
    slot_x = exchange(
        0, slots_out.at[pl.ds(0, cap)], inc.at[pl.ds(0, cap)],
        slots_out.at[pl.ds(cap, cap)], inc.at[pl.ds(2 * cap, cap)],
    )
    rims = tuple(
        exchange(
            1 + i, buf.at[pl.ds(HALO, HALO)], buf.at[pl.ds(HALO + rows_m, HALO)],
            buf.at[pl.ds(rows_m, HALO)], buf.at[pl.ds(0, HALO)],
        )
        for i, buf in enumerate((framed_a, framed_b))
    )

    @pl.when(jnp.logical_not(has_left))
    def _():
        inc[2 * cap : 3 * cap] = jnp.zeros((cap, width), BF16)
        framed_a[0:HALO] = jnp.zeros((HALO, width), BF16)
        framed_b[0:HALO] = jnp.zeros((HALO, width), BF16)

    @pl.when(jnp.logical_not(has_right))
    def _():
        inc[0:cap] = jnp.zeros((cap, width), BF16)
        framed_a[HALO + rows_m :] = jnp.zeros((HALO, width), BF16)
        framed_b[HALO + rows_m :] = jnp.zeros((HALO, width), BF16)

    def pick_rows(target, base, row, first, count):
        column = jnp.broadcast_to(row.astype(F32), (LANES, LANES)).T
        for j in range(count // LANES):
            lane = lax.broadcasted_iota(jnp.int32, (LANES, LANES), 1) + j * LANES
            target[pl.ds(base, LANES), first + j * LANES : first + (j + 1) * LANES] = jnp.where(
                column == lane.astype(F32), 1.0, 0.0
            ).astype(BF16)

    def pick_cols(target, base, row, count):
        sub = lax.broadcasted_iota(jnp.int32, (count, LANES), 0)
        target[:, pl.ds(base, LANES)] = jnp.where(
            sub == jnp.broadcast_to(row, (count, LANES)), 1.0, 0.0
        ).astype(BF16)

    def blocks(count, body):
        def step(e, carry):
            body(e, pl.multiple_of(e * LANES, LANES))
            return carry

        lax.fori_loop(0, count, step, 0)

    def g2m_block(e, base):
        pick_rows(oh_g, base, g2m_s[pl.ds(e, 1), :], 0, oh_g.shape[1])
        pick_cols(oht_q, base, g2m_q[pl.ds(e, 1), :], oht_q.shape[0])

    def mesh_block(e, base):
        row = mesh_r[pl.ds(e, 1), :]
        pick_rows(oh_m, base, mesh_s[pl.ds(e, 1), :], 0, framed_a.shape[0])
        pick_rows(oh_m, base, row, framed_a.shape[0], rows_m)
        pick_cols(oht_m, base, row, rows_m)

    def m2g_block(e, base):
        row = m2g_r[pl.ds(e, 1), :]
        pick_rows(oh_d, base, m2g_s[pl.ds(e, 1), :], 0, framed_a.shape[0])
        pick_rows(oh_d, base, row, framed_a.shape[0], grid.shape[0])
        pick_cols(oht_d, base, row, grid.shape[0])

    def update(v, a, g, names, bias, gain_row):
        message_out, node_in, node_out = (weight(g, m) for m in names)
        incoming = dot(a.astype(BF16), message_out).astype(BF16)
        before = dot(v, node_in[:width]) + dot(incoming, node_in[width:]) + bias[...]
        mixed = dot(silu(before).astype(BF16), node_out)
        centred = mixed - jnp.mean(mixed, axis=1, keepdims=True)
        spread = jnp.mean(centred * centred, axis=1, keepdims=True)
        return (v.astype(F32) + centred * lax.rsqrt(spread + 1e-05) * gain_row[...]).astype(BF16)

    def outer(ref, base=0):
        return jnp.concatenate(
            [ref[base : base + HALO], ref[base + rows_m - HALO : base + rows_m]], axis=0
        )

    def inner(ref, base=0):
        return ref[base + HALO : base + rows_m - HALO]

    def messages(oh, table, count):
        size = 256

        def step(e, carry):
            base = pl.multiple_of(e * size, size)
            msg[pl.ds(base, size), :] = silu(dot(oh[pl.ds(base, size), :], table[...])).astype(BF16)
            return carry

        lax.fori_loop(0, count // size, step, 0)

    z_start(0)
    z_start(1)
    blocks(g2m_s.shape[0], g2m_block)
    z_pass(0)
    counts[...] = dot(oht_q[...], oh_g[...]).astype(BF16)
    for k in range(3):
        pick_cols(land, k * LANES, g2m_l[:, k * LANES : (k + 1) * LANES], rows_m)
    p_pass(0)
    z_pass(1)
    z_start(2)
    blocks(mesh_s.shape[0], mesh_block)
    d_wait(0)
    p_pass(1)
    for copy in states:
        copy.wait()
    hidden = silu(dot(grid[...], weight(0, 0)) + enc_b1[...]).astype(BF16)
    slot_sum = dot(counts[...], hidden).astype(BF16)
    slots_out[0:cap] = slot_sum[0:cap]
    slots_out[cap : 2 * cap] = slot_sum[2 * cap : 3 * cap]
    slot_x[0]()
    inc[cap : 2 * cap] = slot_sum[cap : 2 * cap]
    z_pass(2)
    z_start(3)
    d_wait(1)
    slot_x[1]()
    names = (1, 2, 3)
    arrived = dot(outer(land), inc[...])
    new = update(outer(mesh), arrived, 1, names, enc_nb, enc_gain)
    framed_a[HALO : 2 * HALO] = new[:HALO]
    framed_a[rows_m : HALO + rows_m] = new[HALO:]
    rims[0][0]()
    arrived = dot(inner(land), inc[...])
    framed_a[2 * HALO : rows_m] = update(inner(mesh), arrived, 1, names, enc_nb, enc_gain)
    p_pass(2)
    blocks(m2g_s.shape[0], m2g_block)
    z_pass(3)
    d_wait(2)
    w_in = weight(2, 4)
    own = framed_a[HALO : HALO + rows_m]
    ext = framed_a.shape[0]
    terms[HALO : HALO + rows_m] = dot(own, w_in[:width]).astype(BF16)
    terms[ext:] = (dot(own, w_in[width:]) + proc_b1[...]).astype(BF16)
    rims[0][1]()
    rim = jnp.concatenate([framed_a[0:HALO], framed_a[HALO + rows_m :]], axis=0)
    rim_terms = dot(rim, w_in[:width]).astype(BF16)
    terms[0:HALO] = rim_terms[:HALO]
    terms[HALO + rows_m : ext] = rim_terms[HALO:]
    messages(oh_m, terms, oh_m.shape[0])
    p_pass(3)
    names = (5, 6, 7)
    count = oh_m.shape[0]
    arrived = dot(outer(oht_m), msg[0:count])
    new = update(outer(framed_a, HALO), arrived, 2, names, proc_nb, proc_gain)
    framed_b[HALO : 2 * HALO] = new[:HALO]
    framed_b[rows_m : HALO + rows_m] = new[HALO:]
    rims[1][0]()
    arrived = dot(inner(oht_m), msg[0:count])
    framed_b[2 * HALO : rows_m] = update(
        inner(framed_a, HALO), arrived, 2, names, proc_nb, proc_gain
    )
    d_wait(3)
    w_in = weight(3, 8)
    terms_d[ext:] = (dot(grid[...], w_in[width:]) + dec_b1[...]).astype(BF16)
    terms_d[HALO : HALO + rows_m] = dot(framed_b[HALO : HALO + rows_m], w_in[:width]).astype(BF16)
    rims[1][1]()
    rim = jnp.concatenate([framed_b[0:HALO], framed_b[HALO + rows_m :]], axis=0)
    rim_terms = dot(rim, w_in[:width]).astype(BF16)
    terms_d[0:HALO] = rim_terms[:HALO]
    terms_d[HALO + rows_m : ext] = rim_terms[HALO:]
    messages(oh_d, terms_d, oh_d.shape[0])
    names = (9, 10, 11)
    count = oh_d.shape[0]
    middle = grid.shape[0] // 2
    for lo in (0, middle):
        part = slice(lo, lo + middle)
        arrived = dot(oht_d[part], msg[0:count])
        out_ref[part] = update(grid[part], arrived, 3, names, dec_nb, dec_gain)
    for g in range(4):
        finish(g)
    for moves in (slot_x, *rims):
        moves[2]()


def on_device(
    dims,
    grid_state, mesh_state, g2m_sender, g2m_slot, g2m_land,
    mesh_sender, mesh_receiver, m2g_sender, m2g_receiver,
    enc_msg_w1, enc_msg_b1, enc_msg_w2, enc_node_w1, enc_node_b1, enc_node_w2, enc_gain,
    proc_msg_w1, proc_msg_b1, proc_msg_w2, proc_node_w1, proc_node_b1, proc_node_w2, proc_gain,
    dec_msg_w1, dec_msg_b1, dec_msg_w2, dec_node_w1, dec_node_b1, dec_node_w2, dec_gain,
):
    bands = dims[0]
    weights = (
        enc_msg_w1, enc_msg_w2, enc_node_w1, enc_node_w2,
        proc_msg_w1[0], proc_msg_w2[0], proc_node_w1[0], proc_node_w2[0],
        dec_msg_w1, dec_msg_w2, dec_node_w1, dec_node_w2,
    )
    width = grid_state.shape[1]
    rows_g, rows_m = grid_state.shape[0], mesh_state.shape[0]
    slots = g2m_land.shape[0]
    ext = rows_m + 2 * HALO
    plan = {}
    buffers = []
    for members in GROUPS:
        off = 0
        for m in members:
            rows = weights[m].shape[0]
            plan[m] = (off, rows)
            off += rows
        buffers.append(pltpu.VMEM((bands, -(-off // 32) * 32, width), BF16))
    groups = len(GROUPS)
    e_g, e_m, e_d = g2m_sender.shape[0], mesh_sender.shape[0], m2g_sender.shape[0]
    dma = pltpu.SemaphoreType.DMA
    scratch = buffers + [
        pltpu.VMEM((rows_g, width), BF16),
        pltpu.VMEM((rows_m, width), BF16),
        pltpu.VMEM((slots, width), BF16),
        pltpu.VMEM((2 * slots // 3, width), BF16),
        pltpu.VMEM((ext, width), BF16),
        pltpu.VMEM((ext, width), BF16),
        pltpu.VMEM((slots, rows_g), BF16),
        pltpu.VMEM((e_g, rows_g), BF16),
        pltpu.VMEM((slots, e_g), BF16),
        pltpu.VMEM((rows_m, slots), BF16),
        pltpu.VMEM((e_m, ext + rows_m), BF16),
        pltpu.VMEM((rows_m, e_m), BF16),
        pltpu.VMEM((e_d, ext + rows_g), BF16),
        pltpu.VMEM((rows_g, e_d), BF16),
        pltpu.VMEM((ext + rows_m, width), BF16),
        pltpu.VMEM((ext + rows_g, width), BF16),
        pltpu.VMEM((max(e_m, e_d), width), BF16),
        dma((groups, bands)),
        dma((groups, bands)),
        dma((groups, bands, 3)),
        dma((groups, bands, 3)),
        dma((groups, bands)),
        dma((groups, bands)),
        dma((12,)),
        dma((2,)),
        dma((3, 2)),
        dma((3, 2)),
    ]
    table = lambda v: v.reshape(-1, LANES)
    row = lambda v: v.reshape(1, -1)
    hbm = pl.BlockSpec(memory_space=pl.ANY)
    vmem = pl.BlockSpec(memory_space=pltpu.VMEM)
    return pl.pallas_call(
        functools.partial(kernel, dims, plan),
        out_shape=jax.ShapeDtypeStruct((rows_g, width), BF16),
        in_specs=[hbm] * 2 + [vmem] * 16 + [hbm] * 12,
        out_specs=vmem,
        scratch_shapes=scratch,
        compiler_params=pltpu.CompilerParams(
            collective_id=0, has_side_effects=True, vmem_limit_bytes=52 * 1024 * 1024
        ),
    )(
        grid_state, mesh_state, table(g2m_sender), table(g2m_slot), row(g2m_land),
        table(mesh_sender), table(mesh_receiver), table(m2g_sender), table(m2g_receiver),
        row(enc_msg_b1), row(enc_node_b1), row(enc_gain),
        proc_msg_b1, proc_node_b1, proc_gain,
        row(dec_msg_b1), row(dec_node_b1), row(dec_gain),
        *weights,
    )


def solution(mesh):
    rows = P(("ens", "band", "feat", "sub"), None)
    edges = P(("band", "feat", "sub"))
    flat = P("band", None)
    deep = P(None, "band", None)
    enc = (flat, P(), flat, flat, P(), flat, P())
    proc = (deep, P(), deep, deep, P(), deep, P())
    in_specs = (rows, rows) + (edges,) * 7 + enc + proc + enc
    dims = (mesh.shape["band"], mesh.shape["feat"], mesh.shape["sub"])
    return jax.shard_map(
        functools.partial(on_device, dims),
        mesh=mesh, in_specs=in_specs, out_specs=rows, check_vma=False,
    )
```

time: 288 us -> 94.1 us (0.33)
  blocking collectives: 126 us -> 0 us
  other arithmetic: 76.8 us -> 0 us
  Pallas kernels: 0 us -> 73.1 us
  starting transfers between devices: 33.5 us -> 0 us
  matrix products: 25.8 us -> 0 us
  local copies, waits for them, and re-layouts: 5.63 us -> 19.3 us
  between operations: 13.7 us -> 0.06 us
  waiting for transfers between devices: 5.2 us -> 0 us
    all_gather x7 -> x0, blocking collectives: 126 us -> none  [the longest x3 61.8 us: fetch_section(): lax.all_gather(fourth, 'band', axis=0, tiled=True)]
    scatter-add x4 -> x0, other arithmetic: 74.3 us -> none  [the longest x2 59.6 us: edge_sum(): jax.ops.segment_sum(jax.nn.silu(before), receivers, num_segments=row_count)]
    pallas_call x0 -> x1, Pallas kernels: none -> 73.1 us  [on_device(): pl.pallas_call(functools.partial(kernel, dims, plan), out_shape=jax.Shape...]
    ppermute x6 -> x0, starting transfers between devices: 33.4 us -> none  [the longest x3 21.8 us: with_halo(): lax.ppermute(tail, axis, [(i, (i + 1) % count) for i in range(ends)])]
    dot_general x14 -> x0, matrix products: 25.8 us -> none  [the longest x3 7.8 us: node_update(): jnp.dot(incoming_narrow, node_in[model_width:], preferred_element_type=jn...]
    unnamed x61 -> x51, local copies, waits for them, and re-layouts: 2.96 us -> 18.6 us
  transfers between devices with their start and end apart: 11 -> 0, of which waited for: 1 -> 0; matrix products, arithmetic and copies ran while one was open for 27% -> 0% of each run, Pallas kernels for 0% -> 0%
where the time goes in v1:
time: 94.1 us; the launch traced here: 92.4 us
  Pallas kernels  73.1 us (78%)
  local copies, waits for them, and re-layouts  19.3 us (21%)
    pallas_call x1, Pallas kernels, on_device(): pl.pallas_call(functools.partial(kernel, dims, plan), out_shape=jax.Shape...  73.1 us
    unnamed x51, local copies, waits for them, and re-layouts  18.6 us

profile of v1, /device:TPU:3, one launch (start us, length us, event | category | flops | bytes accessed | tf_op | source)
XLA Modules:
  0.0 92.4 jit_solution(12460359957479893271)
XLA Ops:
  0.0 0.7 reshape.41.refs_4_
  0.8 0.9 %copy-done = bf16[256,512]{1,0:T(8,128)(2,1)S(1)} copy-done((bf16[256,512]{1,0:T(8,128)(2,1)S(1)}, bf16[256,512]{1,0:T(8,128)(2,1)}, u32[]{:S(2)}) %copy-start) | copy-done | bytes 262168
  1.7 0.9 %copy-done.1 = bf16[1,256,512]{2,1,0:T(8,128)(2,1)S(1)} copy-done((bf16[1,256,512]{2,1,0:T(8,128)(2,1)S(1)}, bf16[1,256,512]{2,1,0:T(8,128)(2,1)}, u32[]{:S(2)}) %copy-start.1) | copy-done | bytes 262168
  2.7 0.9 %copy-done.2 = bf16[1,256,512]{2,1,0:T(8,128)(2,1)S(1)} copy-done((bf16[1,256,512]{2,1,0:T(8,128)(2,1)S(1)}, bf16[1,256,512]{2,1,0:T(8,128)(2,1)}, u32[]{:S(2)}) %copy-start.2) | copy-done | bytes 262168
  3.6 0.9 copy-done.3
  4.5 0.9 copy-done.4
  5.4 0.9 copy-done.5
  6.3 0.9 copy-done.6
  7.2 0.9 copy-done.7
  8.1 0.9 copy-done.8
  9.1 0.9 copy-done.9
  10.0 0.7 copy-done.14
  10.6 0.7 copy-done.15
  11.3 0.7 copy-done.16
  12.0 0.7 copy-done.17
  12.7 0.7 copy-done.18
  13.4 0.7 copy-done.19
  14.1 0.7 copy-done.20
  14.7 0.7 copy-done.21
  15.4 0.7 copy-done.22
  16.1 0.7 copy-done.23
  16.8 0.7 copy-done.24
  17.5 73.1 %shard_map.280 = bf16[512,512]{1,0:T(8,128)(2,1)} custom-call(bf16[512,512]{1,0:T(8,128)(2,1)} %refs_0_.1, bf16[512,512]{1,0:T(8,128)(2,1)} %refs_1_.1, s32[8,128]{1,0:T(8,128)S(1)} %bitcast.24, s32[8,128]{1,0:T(8,128)S(1)} %bitcast.25, s32[1,384]{1,0:T(1,128)S(1)} %reshape.41.refs_4_, s32[16,128]{1,0:T(8,128)S(1)} %bitcast.20, s32[16,128]{1,0:T(8,128)S(1)} %bitcast.21, ...), custom_call_target="tpu_custom_call" | custom-call | tf_op jit(solution)/shard_map/pallas_call | solution.py:452
  90.6 1.9 %copy.32 = bf16[512,512]{1,0:T(8,128)(2,1)} copy(bf16[512,512]{1,0:T(8,128)(2,1)} %shard_map.280) | data formatting | bytes 1048576
  (29 shorter events, 0.1 us)
Async XLA Ops:
  0.0 0.7 copy-start.13
  0.0 0.7 copy-start.12
  0.0 0.7 copy-start.10
  0.0 0.8 copy-start.11
  0.8 1.0 %copy-start = (bf16[256,512]{1,0:T(8,128)(2,1)S(1)}, bf16[256,512]{1,0:T(8,128)(2,1)}, u32[]{:S(2)}) copy-start(bf16[256,512]{1,0:T(8,128)(2,1)} %refs_20_.1) | copy-start | bytes 786436
  1.7 0.9 %copy-start.1 = (bf16[1,256,512]{2,1,0:T(8,128)(2,1)S(1)}, bf16[1,256,512]{2,1,0:T(8,128)(2,1)}, u32[]{:S(2)}) copy-start(bf16[1,256,512]{2,1,0:T(8,128)(2,1)} %param.46) | copy-start | bytes 786436
  2.7 0.9 %copy-start.2 = (bf16[1,256,512]{2,1,0:T(8,128)(2,1)S(1)}, bf16[1,256,512]{2,1,0:T(8,128)(2,1)}, u32[]{:S(2)}) copy-start(bf16[1,256,512]{2,1,0:T(8,128)(2,1)} %param.49) | copy-start | bytes 786436
  3.6 0.9 copy-start.3
  4.5 0.9 copy-start.4
  5.4 0.9 copy-start.5
  6.3 0.9 copy-start.6
  7.2 0.9 copy-start.7
  8.1 0.9 copy-start.8
  9.1 0.9 copy-start.9
  10.0 0.7 copy-start.14
  10.6 0.7 copy-start.15
  11.3 0.7 copy-start.16
  12.0 0.7 copy-start.17
  12.7 0.7 copy-start.18
  13.4 0.7 copy-start.19
  14.1 0.7 copy-start.20
  14.7 0.7 copy-start.21
  15.4 0.7 copy-start.22
  16.1 0.7 copy-start.23
  (1 other events, 0.7 us)

commit v2 on v1

--- a/solution.py
+++ b/solution.py
@@ -9,6 +9,7 @@
 
 HALO = 128
 LANES = 128
+VMEM_LIMIT = 60 * 1024 * 1024
 F32 = jnp.float32
 BF16 = jnp.bfloat16
 MESH = pl.DeviceIdType.MESH
@@ -16,6 +17,9 @@
 GROUPS = ((0,), (1, 2, 3), (4, 5, 6, 7), (8, 9, 10, 11))
 
 
+DIRECT = (0,)
+
+
 def silu(v):
     h = 0.5 * v
     return h + h * jnp.tanh(h)
@@ -27,17 +31,20 @@
 
 def kernel(dims, plan, *refs):
     bands, feats, subs = dims
-    (
-        grid_hbm, mesh_hbm, g2m_s, g2m_q, g2m_l, mesh_s, mesh_r, m2g_s, m2g_r,
-        enc_b1, enc_nb, enc_gain, proc_b1, proc_nb, proc_gain, dec_b1, dec_nb, dec_gain,
-    ) = refs[:18]
+    grid_hbm, mesh_hbm = refs[:2]
+    small_hbm = refs[2:18]
     shards = refs[18:30]
     out_ref = refs[30]
     (
         w0, w1, w2, w3, grid, mesh, inc, slots_out, framed_a, framed_b, counts,
         oh_g, oht_q, land, oh_m, oht_m, oh_d, oht_d, terms, terms_d, msg,
-        zsend, zrecv, psend, precv, dsend, drecv, wsem, ssem, hsend, hrecv,
-    ) = refs[31:]
+        zsend, zrecv, psend, precv, fsend, frecv, dsend, drecv,
+        wsem, ssem, nsem, hsend, hrecv,
+    ) = refs[31:-16]
+    (
+        g2m_s, g2m_q, g2m_l, mesh_s, mesh_r, m2g_s, m2g_r,
+        enc_b1, enc_nb, enc_gain, proc_b1, proc_nb, proc_gain, dec_b1, dec_nb, dec_gain,
+    ) = refs[-16:]
     wbufs = (w0, w1, w2, w3)
     y = lax.axis_index("ens")
     z = lax.axis_index("band")
@@ -78,6 +85,12 @@
     for group in local:
         for copy in group:
             copy.start()
+    small = [
+        pltpu.make_async_copy(src, dst, nsem.at[i])
+        for i, (src, dst) in enumerate(zip(small_hbm, refs[-16:]))
+    ]
+    for copy in small:
+        copy.start()
     for copy in states:
         copy.start()
 
@@ -137,18 +150,42 @@
             copy.wait()
         each(lambda r, owner: z_copy(g, r, z, lax.rem(z + r, bands)).start())
 
+    def direct(g):
+        return g in DIRECT
+
+    def f_copy(g, r, owner, i, chunk):
+        quarter = wbufs[g].shape[1] // 4
+        start = pl.multiple_of((2 * c + i) * quarter, 16)
+        piece = wbufs[g].at[owner, pl.ds(start, quarter), cols(chunk)]
+        return pltpu.make_async_remote_copy(
+            piece, piece, fsend.at[g, r, i], frecv.at[g, r, i],
+            device_id=peers[1 - i], device_id_type=MESH,
+        )
+
     def z_pass(g):
         def body(r, owner):
             z_copy(g, r, owner, owner).wait_recv()
-            for j in range(3):
+            for j in range(3 if direct(g) else 2):
                 p_copy(g, r, owner, j, q).start()
+
+        each(body)
+
+    def f_pass(g):
+        def body(r, owner):
+            for i in range(2):
+                p_copy(g, r, owner, i, chunks[i]).wait_recv()
+                f_copy(g, r, owner, i, chunks[i]).start()
 
         each(body)
 
     def p_pass(g):
         def body(r, owner):
-            for j in range(3):
-                p_copy(g, r, owner, j, chunks[j]).wait_recv()
+            if direct(g):
+                for j in range(3):
+                    p_copy(g, r, owner, j, chunks[j]).wait_recv()
+            else:
+                for i in range(2):
+                    f_copy(g, r, owner, i, chunks[2]).wait_recv()
             d_copy(g, r, owner, c).start()
 
         each(body)
@@ -159,8 +196,11 @@
     def finish(g):
         def body(r, owner):
             z_copy(g, r, z, lax.rem(z + r, bands)).wait_send()
-            for j in range(3):
+            for j in range(3 if direct(g) else 2):
                 p_copy(g, r, owner, j, q).wait_send()
+            if not direct(g):
+                for i in range(2):
+                    f_copy(g, r, owner, i, chunks[i]).wait_send()
             d_copy(g, r, owner, c).wait_send()
 
         each(body)
@@ -253,12 +293,12 @@
             sub == jnp.broadcast_to(row, (count, LANES)), 1.0, 0.0
         ).astype(BF16)
 
-    def blocks(count, body):
+    def blocks(first, count, body):
         def step(e, carry):
             body(e, pl.multiple_of(e * LANES, LANES))
             return carry
 
-        lax.fori_loop(0, count, step, 0)
+        lax.fori_loop(first, count, step, 0)
 
     def g2m_block(e, base):
         pick_rows(oh_g, base, g2m_s[pl.ds(e, 1), :], 0, oh_g.shape[1])
@@ -305,27 +345,34 @@
 
     z_start(0)
     z_start(1)
-    blocks(g2m_s.shape[0], g2m_block)
+    for copy in small:
+        copy.wait()
+    blocks(0, g2m_s.shape[0], g2m_block)
     z_pass(0)
+    z_start(2)
     counts[...] = dot(oht_q[...], oh_g[...]).astype(BF16)
     for k in range(3):
-        pick_cols(land, k * LANES, g2m_l[:, k * LANES : (k + 1) * LANES], rows_m)
+        pick_cols(land, k * LANES, g2m_l[k * LANES : (k + 1) * LANES].reshape(1, LANES), rows_m)
     p_pass(0)
     z_pass(1)
-    z_start(2)
-    blocks(mesh_s.shape[0], mesh_block)
-    d_wait(0)
-    p_pass(1)
+    n_m, n_d = mesh_s.shape[0], m2g_s.shape[0]
+    blocks(0, n_m // 4, mesh_block)
     for copy in states:
         copy.wait()
+    d_wait(0)
     hidden = silu(dot(grid[...], weight(0, 0)) + enc_b1[...]).astype(BF16)
     slot_sum = dot(counts[...], hidden).astype(BF16)
     slots_out[0:cap] = slot_sum[0:cap]
     slots_out[cap : 2 * cap] = slot_sum[2 * cap : 3 * cap]
     slot_x[0]()
     inc[cap : 2 * cap] = slot_sum[cap : 2 * cap]
+    f_pass(1)
     z_pass(2)
     z_start(3)
+    blocks(n_m // 4, n_m // 2, mesh_block)
+    p_pass(1)
+    blocks(n_m // 2, n_m, mesh_block)
+    f_pass(2)
     d_wait(1)
     slot_x[1]()
     names = (1, 2, 3)
@@ -334,11 +381,12 @@
     framed_a[HALO : 2 * HALO] = new[:HALO]
     framed_a[rows_m : HALO + rows_m] = new[HALO:]
     rims[0][0]()
+    z_pass(3)
+    p_pass(2)
     arrived = dot(inner(land), inc[...])
     framed_a[2 * HALO : rows_m] = update(inner(mesh), arrived, 1, names, enc_nb, enc_gain)
-    p_pass(2)
-    blocks(m2g_s.shape[0], m2g_block)
-    z_pass(3)
+    blocks(0, n_d, m2g_block)
+    f_pass(3)
     d_wait(2)
     w_in = weight(2, 4)
     own = framed_a[HALO : HALO + rows_m]
@@ -412,7 +460,7 @@
             rows = weights[m].shape[0]
             plan[m] = (off, rows)
             off += rows
-        buffers.append(pltpu.VMEM((bands, -(-off // 32) * 32, width), BF16))
+        buffers.append(pltpu.VMEM((bands, -(-off // 64) * 64, width), BF16))
     groups = len(GROUPS)
     e_g, e_m, e_d = g2m_sender.shape[0], mesh_sender.shape[0], m2g_sender.shape[0]
     dma = pltpu.SemaphoreType.DMA
@@ -438,33 +486,39 @@
         dma((groups, bands)),
         dma((groups, bands, 3)),
         dma((groups, bands, 3)),
+        dma((groups, bands, 2)),
+        dma((groups, bands, 2)),
         dma((groups, bands)),
         dma((groups, bands)),
         dma((12,)),
         dma((2,)),
+        dma((16,)),
         dma((3, 2)),
         dma((3, 2)),
     ]
     table = lambda v: v.reshape(-1, LANES)
     row = lambda v: v.reshape(1, -1)
-    hbm = pl.BlockSpec(memory_space=pl.ANY)
+    small = (
+        table(g2m_sender), table(g2m_slot), g2m_land,
+        table(mesh_sender), table(mesh_receiver), table(m2g_sender), table(m2g_receiver),
+        row(enc_msg_b1), row(enc_node_b1), row(enc_gain),
+        proc_msg_b1, proc_node_b1, proc_gain,
+        row(dec_msg_b1), row(dec_node_b1), row(dec_gain),
+    )
+    scratch += [pltpu.VMEM(v.shape, v.dtype) for v in small]
+    hbm = pl.BlockSpec(memory_space=pltpu.HBM)
     vmem = pl.BlockSpec(memory_space=pltpu.VMEM)
     return pl.pallas_call(
         functools.partial(kernel, dims, plan),
         out_shape=jax.ShapeDtypeStruct((rows_g, width), BF16),
-        in_specs=[hbm] * 2 + [vmem] * 16 + [hbm] * 12,
+        in_specs=[hbm] * 30,
         out_specs=vmem,
         scratch_shapes=scratch,
         compiler_params=pltpu.CompilerParams(
-            collective_id=0, has_side_effects=True, vmem_limit_bytes=52 * 1024 * 1024
+            collective_id=0, has_side_effects=True, vmem_limit_bytes=VMEM_LIMIT
         ),
     )(
-        grid_state, mesh_state, table(g2m_sender), table(g2m_slot), row(g2m_land),
-        table(mesh_sender), table(mesh_receiver), table(m2g_sender), table(m2g_receiver),
-        row(enc_msg_b1), row(enc_node_b1), row(enc_gain),
-        proc_msg_b1, proc_node_b1, proc_gain,
-        row(dec_msg_b1), row(dec_node_b1), row(dec_gain),
-        *weights,
+        grid_state, mesh_state, *small, *weights
     )
 
 

time: 94.1 us -> 66.5 us (0.71)
  local copies, waits for them, and re-layouts: 19.3 us -> 1.87 us
  Pallas kernels: 73.1 us -> 63.5 us
    unnamed x51 -> x1, local copies, waits for them, and re-layouts: 18.6 us -> 1.87 us
    pallas_call x1, Pallas kernels: 73.1 us -> 63.5 us  [on_device(): pl.pallas_call(functools.partial(kernel, dims, plan), out_shape=jax.Shape...]
where the time goes in v2:
time: 66.5 us; the launch traced here: 65.4 us
  Pallas kernels  63.5 us (95%)
  local copies, waits for them, and re-layouts  1.87 us (3%)
    pallas_call x1, Pallas kernels, on_device(): pl.pallas_call(functools.partial(kernel, dims, plan), out_shape=jax.Shape...  63.5 us
    unnamed x1, local copies, waits for them, and re-layouts  1.87 us

profile of v2, /device:TPU:3, one launch (start us, length us, event | category | flops | bytes accessed | tf_op | source)
XLA Modules:
  0.0 65.4 jit_solution(11481169214929535274)
XLA Ops:
  0.0 63.5 %shard_map.280 = bf16[512,512]{1,0:T(8,128)(2,1)} custom-call(bf16[512,512]{1,0:T(8,128)(2,1)} %refs_0_.1, bf16[512,512]{1,0:T(8,128)(2,1)} %refs_1_.1, s32[8,128]{1,0:T(8,128)} %bitcast.24, s32[8,128]{1,0:T(8,128)} %bitcast.25, s32[384]{0:T(512)} %refs_4_.1, s32[16,128]{1,0:T(8,128)} %bitcast.20, s32[16,128]{1,0:T(8,128)} %bitcast.21, s32[12,128]{1,0:T(8,128)} %bitcast.22, ...), custom_call_target="tpu_custom_call" | custom-call | tf_op jit(solution)/shard_map/pallas_call | solution.py:511
  63.5 1.9 %copy.32 = bf16[512,512]{1,0:T(8,128)(2,1)} copy(bf16[512,512]{1,0:T(8,128)(2,1)} %shard_map.280) | data formatting | bytes 1048576

commit v3 on v2

--- a/solution.py
+++ b/solution.py
@@ -373,6 +373,7 @@
     p_pass(1)
     blocks(n_m // 2, n_m, mesh_block)
     f_pass(2)
+    blocks(0, n_d, m2g_block)
     d_wait(1)
     slot_x[1]()
     names = (1, 2, 3)
@@ -385,7 +386,6 @@
     p_pass(2)
     arrived = dot(inner(land), inc[...])
     framed_a[2 * HALO : rows_m] = update(inner(mesh), arrived, 1, names, enc_nb, enc_gain)
-    blocks(0, n_d, m2g_block)
     f_pass(3)
     d_wait(2)
     w_in = weight(2, 4)

time: 66.5 us -> 67.4 us (1.014); the launches traced: 65.4 us -> 67.2 us
  Pallas kernels: 63.5 us -> 65.4 us
    pallas_call x1, Pallas kernels: 63.5 us -> 65.4 us  [on_device(): pl.pallas_call(functools.partial(kernel, dims, plan), out_shape=jax.Shape...]
where the time goes in v3:
time: 67.4 us; the launch traced here: 67.2 us
  Pallas kernels  65.4 us (97%)
  local copies, waits for them, and re-layouts  1.87 us (3%)
    pallas_call x1, Pallas kernels, on_device(): pl.pallas_call(functools.partial(kernel, dims, plan), out_shape=jax.Shape...  65.4 us
    unnamed x1, local copies, waits for them, and re-layouts  1.87 us

profile of v3, /device:TPU:3, one launch (start us, length us, event | category | flops | bytes accessed | tf_op | source)
XLA Modules:
  0.0 67.2 jit_solution(11104508268934768214)
XLA Ops:
  0.0 65.4 %shard_map.280 = bf16[512,512]{1,0:T(8,128)(2,1)} custom-call(bf16[512,512]{1,0:T(8,128)(2,1)} %refs_0_.1, bf16[512,512]{1,0:T(8,128)(2,1)} %refs_1_.1, s32[8,128]{1,0:T(8,128)} %bitcast.24, s32[8,128]{1,0:T(8,128)} %bitcast.25, s32[384]{0:T(512)} %refs_4_.1, s32[16,128]{1,0:T(8,128)} %bitcast.20, s32[16,128]{1,0:T(8,128)} %bitcast.21, s32[12,128]{1,0:T(8,128)} %bitcast.22, ...), custom_call_target="tpu_custom_call" | custom-call | tf_op jit(solution)/shard_map/pallas_call | solution.py:511
  65.4 1.9 %copy.32 = bf16[512,512]{1,0:T(8,128)(2,1)} copy(bf16[512,512]{1,0:T(8,128)(2,1)} %shard_map.280) | data formatting | bytes 1048576
